TPU v7x, 1024 devices: a whole 8x8x8 slice. The times are simulated.
1024 devices in a mesh: dp: 64 (over x, z), fsdp: 16 (over y, core).
Axes of the slice: x: 8, y: 8, z: 8, core: 2. Of those that a mesh axis runs over, the one named last changes fastest.
Arguments:
- attn: bfloat16 [64, 2, 1024, 4096], P('dp', None, 'fsdp')
- resid: bfloat16 [64, 2, 1024, 4096], P('dp', None, 'fsdp')
- lengths: int32 [64, 2], P('dp'), may hold values from 1 to 1024, as said below
- out_proj: bfloat16 [4096, 4096], P('fsdp'), may hold values from -0.09375 to 0.09375
- norm_gain: float32 [4096], replicated, may hold values from 0.5 to 1.5
- bank: bfloat16 [128, 4096], P('dp'), may hold values from -6 to 6
- hard_ids: int32 [64, 8], replicated, may hold values from 0 to 127
Outputs:
- loss: float32 [], replicated
- grad_out_proj: float32 [4096, 4096], P('dp', 'fsdp')
Inputs may be any that keep to these rules, and one draw needn't show every extreme that they name: The pooled position of a sequence is its last one, lengths - 1.
All inputs are finite; a program needn't handle non-finite values.
Results may differ from a plain program's by a relative error of at most 0.0052.
Values may be sent and summed in bfloat16 or wider, within the bound.
A program may use at most 32 MiB of HBM per device.

v0:
```python
import math

import jax
import jax.numpy as jnp
from jax import lax
from jax.sharding import PartitionSpec as P


def pick_last(values, lengths, offset):
    local_len = values.shape[2]
    places = jnp.arange(local_len, dtype=jnp.int32)[None, None, :] + offset
    select = (places == (lengths - 1)[:, :, None]).astype(values.dtype)
    return jnp.einsum("skl,skld->skd", select, values, preferred_element_type=jnp.float32)


def on_device(attn, resid, lengths, out_proj, norm_gain, bank, hard_ids):
    seq_dev, kinds, local_len, width = attn.shape
    block = out_proj.shape[0]
    shard = lax.axis_index("fsdp")
    own_attn = pick_last(attn, lengths, shard * local_len).astype(jnp.bfloat16)
    own_resid = pick_last(resid, lengths, shard * local_len).astype(jnp.bfloat16)
    pooled_attn, pooled_resid = (
        lax.psum(own_attn, "fsdp").astype(jnp.float32),
        lax.psum(own_resid, "fsdp").astype(jnp.float32),
    )
    attn_rows = pooled_attn.astype(jnp.bfloat16).reshape(seq_dev * kinds, width)
    columns = lax.dynamic_slice_in_dim(attn_rows, shard * block, block, 1)
    partial_out = jnp.dot(columns, out_proj, preferred_element_type=jnp.float32)
    projected = lax.psum(partial_out, "fsdp")
    hidden = pooled_resid.reshape(seq_dev * kinds, width) + projected
    inv_rms = lax.rsqrt(jnp.mean(hidden * hidden, axis=-1, keepdims=True) + 1e-05)
    normed = hidden * inv_rms
    embedded = (normed * norm_gain).astype(jnp.bfloat16)
    every_emb, every_bank = (
        lax.all_gather(embedded, "dp", axis=0, tiled=True),
        lax.all_gather(bank, "dp", axis=0, tiled=True),
    )
    pairs = every_emb.reshape(-1, 2, width)
    queries = pairs[:, 0]
    passages = pairs[:, 1]
    count = queries.shape[0]
    scale = 4.0 / math.sqrt(width)
    scores = jnp.dot(queries, passages.T, preferred_element_type=jnp.float32) * scale
    bank_scores = jnp.dot(queries, every_bank.T, preferred_element_type=jnp.float32) * scale
    bank_rows = every_bank.shape[0]
    onehot = (hard_ids[:, :, None] == jnp.arange(bank_rows, dtype=jnp.int32)[None, None, :]).astype(
        jnp.float32
    )
    hard = jnp.einsum("shn,sn->sh", onehot, bank_scores, precision=lax.Precision.HIGHEST)
    row_lse = jax.nn.logsumexp(jnp.concatenate([scores, hard], axis=1), axis=1)
    col_lse = jax.nn.logsumexp(scores, axis=0)
    diag = jnp.diagonal(scores)
    loss = (jnp.sum(row_lse - diag) + jnp.sum(col_lse - diag)) / (2.0 * count)
    eye = jnp.eye(count, dtype=jnp.float32)
    dscore = (
        jnp.exp(scores - row_lse[:, None]) + jnp.exp(scores - col_lse[None, :]) - 2.0 * eye
    ) / (2.0 * count)
    dhard = jnp.exp(hard - row_lse[:, None]) / (2.0 * count)
    bank_weight = jnp.einsum("shn,sh->sn", onehot, dhard, precision=lax.Precision.HIGHEST)
    first = lax.axis_index("dp") * seq_dev
    row_ds = lax.dynamic_slice_in_dim(dscore, first, seq_dev, 0)
    col_ds = lax.dynamic_slice_in_dim(dscore, first, seq_dev, 1)
    row_bank = lax.dynamic_slice_in_dim(bank_weight, first, seq_dev, 0)
    grad_query = jnp.dot(row_ds, passages.astype(jnp.float32), precision=lax.Precision.HIGHEST)
    grad_query = (
        grad_query
        + jnp.dot(row_bank, every_bank.astype(jnp.float32), precision=lax.Precision.HIGHEST)
    ) * scale
    grad_passage = (
        jnp.dot(col_ds.T, queries.astype(jnp.float32), precision=lax.Precision.HIGHEST) * scale
    )
    grad_emb = jnp.stack([grad_query, grad_passage], axis=1).reshape(seq_dev * kinds, width)
    dz = grad_emb * norm_gain
    centre = jnp.mean(normed * dz, axis=-1, keepdims=True)
    grad_hidden = inv_rms * (dz - normed * centre)
    grad_cols = lax.dynamic_slice_in_dim(grad_hidden, shard * block, block, 1)
    attn_float = attn_rows.astype(jnp.float32)
    grad_out_proj = lax.psum_scatter(
        jnp.dot(attn_float.T, grad_cols, precision=lax.Precision.HIGHEST),
        "dp",
        scatter_dimension=0,
        tiled=True,
    )
    return (loss, grad_out_proj)


def solution(mesh):
    placed = (
        P("dp", None, "fsdp", None),
        P("dp", None, "fsdp", None),
        P("dp", None),
        P("fsdp", None),
        P(),
        P("dp", None),
        P(),
    )
    return jax.shard_map(
        on_device, mesh=mesh, in_specs=placed, out_specs=(P(), P("dp", "fsdp")), check_vma=False
    )
```

profile of v0, /device:TPU:1, one launch (start us, length us, event | category | flops | bytes accessed | tf_op | source)
XLA Modules:
  0.0 478.0 jit_solution(16040956054131924999)
XLA Ops:
  7.2 0.7 all-gather.7.cloned.1.call-update
  8.0 0.7 add_bitcast_fusion
  8.7 1.5 fusion
  10.3 1.5 fusion.2
  11.8 56.8 %all-reduce = (bf16[1,2,4096]{2,1,0:T(2,128)(2,1)S(1)}, bf16[2,4096]{1,0:T(2,128)(2,1)S(1)}) all-reduce(bf16[1,2,4096]{2,1,0:T(2,128)(2,1)S(1)} %bitcast.87, bf16[2,4096]{1,0:T(2,128)(2,1)S(1)} %bitcast.89), channel_id=1, replica_groups=mesh['dp'=64,'fsdp'=16] {'fsdp'}, use_global_device_ids=true, to_apply=%region_1.0 | all-reduce | flops 16384 | bytes 65536 | tf_op jit(solution)/shard_map/psum | solution.py:23
  68.5 0.4 fusion.25
  68.9 46.1 %psum.23 = f32[2,4096]{1,0:T(2,128)S(1)} all-reduce(f32[2,4096]{1,0:T(2,128)S(1)} %fusion.25), channel_id=1, replica_groups=mesh['dp'=64,'fsdp'=16] {'fsdp'}, use_global_device_ids=true, to_apply=%region_2.0 | all-reduce | flops 8192 | bytes 65536 | tf_op jit(solution)/shard_map/psum | solution.py:29
  115.0 0.1 multiply_reduce_fusion.1
  115.2 0.7 fusion.13
  115.9 0.1 copy.13
  116.1 1.5 reshape.148
  117.5 85.4 %all-gather.5.cloned.1.call-done = bf16[64,2,4096]{2,1,0:T(2,128)(2,1)} async-done(((bf16[1,2,4096]{2,1,0:T(2,128)(2,1)}), bf16[64,2,4096]{2,1,0:T(2,128)(2,1)}) %all-gather.5.cloned.1.call-update) | async-done | bytes 1048592 | tf_op jit(solution)/shard_map/all_gather | solution.py:35
  203.0 3.6 fusion.36
  206.6 0.8 convolution_multiply_fusion
  207.4 0.2 copy-done.1
  207.6 1.2 fusion.37
  208.8 0.8 gather_fusion
  209.6 0.1 exponential_reduce_fusion
  209.7 0.4 fusion.5
  210.2 0.1 reduce_max.34
  210.3 0.2 fusion.10
  210.5 0.6 subtract_reduce_fusion
  211.1 0.1 subtract_multiply_fusion
  211.2 2.0 fusion.6
  213.2 0.2 dynamic-slice_reduce_fusion
  213.4 0.1 exponential_multiply_fusion
  213.5 2.0 fusion.32
  215.6 0.4 fusion.4
  216.0 0.5 fusion.30
  216.5 0.2 multiply_reduce_fusion
  216.7 3.8 fusion.15
  221.8 248.6 %reduce-scatter.2.cloned.1.call-done = f32[64,256]{1,0:T(8,128)} async-done(((f32[4096,256]{1,0:T(8,128)}), f32[64,256]{1,0:T(8,128)}) %reduce-scatter.2.cloned.1.call-update) | async-done | bytes 65552 | tf_op jit(solution)/shard_map/reduce_scatter | solution.py:78
  (26 shorter events, 0.4 us)
Async XLA Ops:
  7.2 61.4 %copy-start = (bf16[256,4096]{1,0:T(8,128)(2,1)S(1)}, bf16[256,4096]{1,0:T(8,128)(2,1)}, u32[]{:S(2)}) copy-start(bf16[256,4096]{1,0:T(8,128)(2,1)} %param.10) | copy-start | bytes 6291460
  7.2 108.9 %all-gather.7.cloned.1.call-start = ((), (), s32[]{:S(2)}) async-start(), calls=%async_computation.3 | async-start | bytes 1064960 | tf_op jit(solution)/shard_map/all_gather | solution.py:36
  7.9 195.1 %all-gather.5.cloned.1.call-start = ((), (), s32[]{:S(2)}) async-start(), calls=%async_computation.2 | async-start | bytes 1064960 | tf_op jit(solution)/shard_map/all_gather | solution.py:35
  8.7 106.4 %copy-start.3 = (f32[4096]{0:T(1024)S(1)}, f32[4096]{0:T(1024)}, u32[]{:S(2)}) copy-start(f32[4096]{0:T(1024)} %param.11) | copy-start | bytes 49156
  8.7 107.2 %copy-start.4 = (s32[64,8]{0,1:T(8,128)S(1)}, s32[64,8]{0,1:T(8,128)}, u32[]{:S(2)}) copy-start(s32[64,8]{0,1:T(8,128)} %param.13) | copy-start | bytes 6148
  115.9 354.5 %reduce-scatter.2.cloned.1.call-start = ((), (), s32[]{:S(2)}) async-start(), calls=%async_computation.1 | async-start | bytes 4259840 | tf_op jit(solution)/shard_map/reduce_scatter | solution.py:78
  206.6 1.0 copy-start.1
  206.6 2.2 copy-start.2
Sparse Core Ops, SparseCore 0:
  12.2 97.3 all-gather.6
  116.0 86.9 all-gather.4
  220.6 249.6 reduce-scatter.1
where the time goes:
time: 482 us; the launch traced here: 478 us
  waiting for transfers between devices  335 us (70%)
  blocking collectives  103 us (21%)
  between operations  16.3 us (3%)
  matrix products  14.6 us (3%)
  local copies, waits for them, and re-layouts  6.38 us (1%)
    reduce_scatter x1, waiting for transfers between devices, on_device(): lax.psum_scatter(jnp.dot(attn_float.T, grad_cols, precision=lax.Precision...  249 us
    all_gather x1, waiting for transfers between devices, on_device(): lax.all_gather(embedded, 'dp', axis=0, tiled=True)  85.4 us
    psum x1, blocking collectives, on_device(): lax.psum(own_attn, 'fsdp').astype(jnp.float32)  56.8 us
    psum x1, blocking collectives, on_device(): projected = lax.psum(partial_out, 'fsdp')  46.1 us
  transfers between devices with their start and end apart: 3, of which 2 were waited for; matrix products, arithmetic and copies ran while one was open for 1% of the time, Pallas kernels for 0%

commit v1 on v0

v1 whole, which is shorter than its diff:
```python
import jax
import jax.numpy as jnp
from jax import lax
from jax.experimental import pallas as pl
from jax.experimental.pallas import tpu as pltpu
from jax.sharding import PartitionSpec as P

MESH = pl.DeviceIdType.MESH
F32 = jnp.float32
BF16 = jnp.bfloat16

SIDE = 8
DP = 64
FS = 16
D = 4096
BLK = 256
SCALE = 4.0 / 64.0
COUNT = 128.0

ATTN, RESID, BANK, COLS, PAIR, YSUM, SQ, NORM, INV, RELAY, SPAIR, SY, SBACK = range(13)
KINDS = 13


def far(m):
    return lax.rem(12 + (2 * lax.rem(m, 2) - 1) * lax.div(m + 1, 2), SIDE)


def dot(a, b, ca, cb):
    return lax.dot_general(a, b, (((ca,), (cb,)), ((), ())), preferred_element_type=F32)


def dot2(a, b, ca, cb):
    hi = a.astype(BF16)
    lo = (a - hi.astype(F32)).astype(BF16)
    return dot(hi, b, ca, cb) + dot(lo, b, ca, cb)


def kernel(
    attn, resid, lengths, w, gain, bank, ids, loss_out, grad_out,
    attn_v, resid_v, len_s, w_v, gain_v, bank_v, ids_v,
    src1, rcv1, lhs, part, cbuf, half, ybuf, hid, sq, sqr,
    nsrc, nbuf, isrc, ibuf, bsrc, bbuf, asrc, abuf, at_full, at_buf,
    pay, cb4, half4, yb4, tot, flat, local_sem, ssem, rsem,
):
    i = lax.axis_index("dp")
    j = lax.axis_index("fsdp")
    x, z = lax.div(i, SIDE), lax.rem(i, SIDE)
    y, c = lax.div(j, 2), lax.rem(j, 2)
    partner = (i, 2 * y + 1 - c)

    def dp_peer(t):
        px = lax.rem(x + far(lax.div(t, SIDE)), SIDE)
        pz = lax.rem(z + far(lax.rem(t, SIDE)), SIDE)
        return (px * SIDE + pz, j)

    def fs_index(t):
        return 2 * lax.rem(y + far(lax.div(t, 2)), SIDE) + lax.rem(c + t + 1, 2)

    def y_peer(t):
        return (i, 2 * lax.rem(y + far(t), SIDE) + c)

    def send(src, dst, kind, to):
        pltpu.make_async_remote_copy(
            src_ref=src, dst_ref=dst, send_sem=ssem.at[kind], recv_sem=rsem.at[kind],
            device_id=to, device_id_type=MESH,
        ).start()

    def arrived(ref, kind):
        pltpu.make_async_copy(ref, ref, rsem.at[kind]).wait()

    def sent(ref, kind):
        pltpu.make_async_copy(ref, ref, ssem.at[kind]).wait()

    loads = [
        pltpu.make_async_copy(a, b, local_sem.at[n])
        for n, (a, b) in enumerate([
            (lengths, len_s), (attn.at[0], attn_v), (resid.at[0], resid_v), (bank, bank_v),
            (ids, ids_v), (gain, gain_v), (w, w_v),
        ])
    ]
    for load in loads:
        load.start()

    barrier = pltpu.get_barrier_semaphore()

    @pl.loop(0, DP - 1)
    def _(t):
        pl.semaphore_signal(barrier, inc=1, device_id=dp_peer(t), device_id_type=MESH)

    @pl.loop(0, FS - 1)
    def _(t):
        pl.semaphore_signal(barrier, inc=1, device_id=(i, fs_index(t)), device_id_type=MESH)

    loads[0].wait()
    loads[1].wait()
    row = lax.broadcasted_iota(jnp.int32, (16, 128), 0)
    col = lax.broadcasted_iota(jnp.int32, (16, 128), 1)
    place_q = len_s[0, 0] - 1 - 64 * j
    place_p = len_s[0, 1] - 1 - 64 * j
    pick = jnp.where(
        row < 2,
        jnp.where(col < 64, col, -1) - place_q,
        jnp.where(col >= 64, col - 64, -1) - place_p,
    )
    inside = jnp.where(row < 2, jnp.where(col < 64, 1, 0), jnp.where(col >= 64, 1, 0))
    select = jnp.where((pick == 0) & (inside == 1), 1.0, 0.0).astype(BF16)
    even = lax.rem(row, 2) == 0

    def fold(block):
        return jnp.where(even, block[:, :128], block[:, 128:])[0:4]

    for t in range(FS):
        src1[0, t] = fold(dot(select, attn_v[:, :, t * BLK:(t + 1) * BLK].reshape(128, BLK), 1, 0))
    rcv1[0, j] = src1[0, j]
    pl.semaphore_wait(barrier, DP - 1 + FS - 1)

    @pl.loop(0, FS - 1)
    def _(t):
        to = fs_index(t)
        send(src1.at[0, to], rcv1.at[0, j], ATTN, (i, to))

    loads[2].wait()
    for t in range(FS):
        src1[1, t] = fold(dot(select, resid_v[:, :, t * BLK:(t + 1) * BLK].reshape(128, BLK), 1, 0))
    rcv1[1, j] = src1[1, j]

    @pl.loop(0, FS - 1)
    def _(t):
        to = fs_index(t)
        send(src1.at[1, to], rcv1.at[1, j], RESID, (i, to))

    loads[3].wait()
    own = pl.ds(pl.multiple_of(j * BLK, BLK), BLK)
    bank_rows = bank_v[:, own].astype(F32)
    bsrc[0:1] = bank_rows[0:1, :128]
    bsrc[1:2] = bank_rows[0:1, 128:]
    bsrc[2:3] = bank_rows[1:2, :128]
    bsrc[3:4] = bank_rows[1:2, 128:]
    bbuf[i] = bsrc[...]

    @pl.loop(0, DP - 1)
    def _(t):
        send(bsrc, bbuf.at[i], BANK, dp_peer(t))

    lhs[...] = jnp.zeros_like(lhs)
    loads[6].wait()

    arrived(rcv1.at[0, pl.ds(0, FS - 1)], ATTN)
    block = jnp.sum(rcv1[0], axis=0)
    asrc[...] = block
    for r in range(4):
        lhs[r:r + 1, 0:128] = block[r - r % 2:r - r % 2 + 1]
        lhs[r:r + 1, 128:256] = block[r - r % 2 + 1:r - r % 2 + 2]
    rows = lhs[...].astype(BF16)
    for t in range(FS):
        part[t % 2, t // 2] = fold(dot(rows, w_v[:, t * BLK:(t + 1) * BLK], 1, 0))
    arrived(rcv1.at[1, pl.ds(0, FS - 1)], RESID)
    part[c, y] = part[c, y] + jnp.sum(rcv1[1], axis=0)
    send(part.at[1 - c], cbuf, PAIR, partner)

    @pl.loop(0, 4)
    def _(t):
        to = 4 * j + t

        @pl.when(to != i)
        def _():
            send(asrc, abuf.at[i], COLS, (to, j))

    relay = lax.div(i, 4)

    @pl.when(relay == j)
    def _():
        abuf[i] = asrc[...]

    arrived(cbuf, PAIR)
    half[...] = part[c] + cbuf[...]
    ybuf[y] = half[...]

    @pl.loop(0, SIDE - 1)
    def _(t):
        send(half, ybuf.at[y], YSUM, y_peer(t))

    loads[4].wait()
    loads[5].wait()
    eye = lax.broadcasted_iota(jnp.int32, (64, 64), 0) == lax.broadcasted_iota(jnp.int32, (64, 64), 1)
    eye_f = jnp.where(eye, 1.0, 0.0)
    ids_t = ids_v[...]
    spot = lax.rem(ids_t, 2) * 64 + lax.div(ids_t, 2)
    bank_row = lax.broadcasted_iota(jnp.int32, (128, 64), 0)

    arrived(ybuf.at[pl.ds(0, SIDE - 1)], YSUM)
    hid[...] = jnp.sum(ybuf[...], axis=0)
    sq[...] = jnp.sum(hid[...] * hid[...], axis=0)
    send(sq, sqr, SQ, partner)
    arrived(sqr, SQ)
    sums = jnp.sum(sq[...] + sqr[...], axis=1, keepdims=True)
    inv_q = lax.rsqrt((sums[0:1] + sums[1:2]) * (1.0 / D) + 1e-5)
    inv_p = lax.rsqrt((sums[2:3] + sums[3:4]) * (1.0 / D) + 1e-5)
    four = lax.broadcasted_iota(jnp.int32, (4, 128), 0)
    nsrc[...] = hid[y] * jnp.where(four < 2, inv_q, inv_p)
    lane = lax.broadcasted_iota(jnp.int32, (1, 128), 1)
    isrc[...] = jnp.where(lane < 64, inv_q, inv_p)

    @pl.loop(0, DP - 1)
    def _(t):
        send(nsrc, nbuf.at[i], NORM, dp_peer(t))

    nbuf[i] = nsrc[...]
    ibuf[i] = isrc[...]

    @pl.loop(0, DP - 1)
    def _(t):
        send(isrc, ibuf.at[i], INV, dp_peer(t))

    @pl.when(relay == j)
    def _():
        arrived(abuf.at[pl.ds(0, DP - 1)], COLS)
        low = lax.rem(i, 4) < 2
        rows_q = jnp.where(low, abuf[:, 0, :], abuf[:, 1, :])
        rows_p = jnp.where(low, abuf[:, 2, :], abuf[:, 3, :])
        at_full[...] = jnp.concatenate([rows_q, rows_p], axis=0).T.astype(BF16)
        mine = pl.ds(pl.multiple_of(lax.rem(i, 2) * 64, 64), 64)
        at_buf[...] = at_full[mine, :]

        @pl.loop(0, FS - 1)
        def _(t):
            send(at_full.at[mine], at_buf, RELAY, (i, fs_index(t)))

    arrived(bbuf.at[pl.ds(0, DP - 1)], BANK)
    bank_e = jnp.concatenate([bbuf[:, 0, :], bbuf[:, 1, :]], axis=1).astype(BF16)
    bank_o = jnp.concatenate([bbuf[:, 2, :], bbuf[:, 3, :]], axis=1).astype(BF16)
    g = gain_v[:, own]

    arrived(nbuf.at[pl.ds(0, DP - 1)], NORM)
    nq = jnp.concatenate([nbuf[:, 0, :], nbuf[:, 1, :]], axis=1)
    np_ = jnp.concatenate([nbuf[:, 2, :], nbuf[:, 3, :]], axis=1)
    eq = (nq * g).astype(BF16)
    ep = (np_ * g).astype(BF16)
    right = jnp.concatenate([ep, bank_e, bank_o], axis=0)
    st = dot(right, eq, 1, 1)
    bank_st = st[64:192]
    flat[0:32, 0:64] = st[0:32]
    flat[0:32, 64:128] = st[32:64]
    flat[32:40, :] = jnp.zeros((8, 128), F32)
    for h in range(8):
        hit = jnp.where(bank_row == spot[h:h + 1], bank_st, 0.0)
        flat[32 + h:33 + h, 0:64] = jnp.sum(hit, axis=0, keepdims=True)
    for k in range(10):
        pay[k // 5, k % 5] = flat[4 * k:4 * k + 4]
    send(pay.at[1 - c], cb4, SPAIR, partner)
    arrived(cb4, SPAIR)
    half4[...] = pay[c] + cb4[...]
    yb4[y] = half4[...]

    @pl.loop(0, SIDE - 1)
    def _(t):
        send(half4, yb4.at[y], SY, y_peer(t))

    arrived(yb4.at[pl.ds(0, SIDE - 1)], SY)
    tot[c] = jnp.sum(yb4[...], axis=0)
    send(tot.at[c], tot.at[c], SBACK, partner)
    arrived(tot.at[0], SBACK)
    for k in range(10):
        flat[4 * k:4 * k + 4] = tot[k // 5, k % 5]
    scores = jnp.concatenate([flat[0:32, 0:64], flat[0:32, 64:128]], axis=0) * SCALE
    hard = flat[32:40, 0:64] * SCALE

    top = jnp.maximum(jnp.max(scores, axis=0, keepdims=True), jnp.max(hard, axis=0, keepdims=True))
    row_lse = top + jnp.log(
        jnp.sum(jnp.exp(scores - top), axis=0, keepdims=True)
        + jnp.sum(jnp.exp(hard - top), axis=0, keepdims=True)
    )
    peak = jnp.max(scores, axis=1, keepdims=True)
    col_lse = peak + jnp.log(jnp.sum(jnp.exp(scores - peak), axis=1, keepdims=True))
    diag = jnp.sum(jnp.where(eye, scores, 0.0), axis=1, keepdims=True)
    loss_out[...] = (
        jnp.sum(row_lse, axis=1, keepdims=True)
        + jnp.sum(col_lse - 2.0 * diag, axis=0, keepdims=True)
    ) * (1.0 / COUNT)
    dscore = (jnp.exp(scores - row_lse) + jnp.exp(scores - col_lse) - 2.0 * eye_f) * (1.0 / COUNT)
    dhard = jnp.exp(hard - row_lse) * (1.0 / COUNT)
    weight = jnp.zeros((128, 64), F32)
    for h in range(8):
        weight = weight + jnp.where(bank_row == spot[h:h + 1], dhard[h:h + 1], 0.0)
    weighted = dscore * scores
    centre_p = jnp.sum(weighted, axis=1, keepdims=True) * (1.0 / D)
    centre_row = (
        jnp.sum(weighted, axis=0, keepdims=True) + jnp.sum(dhard * hard, axis=0, keepdims=True)
    ) * (1.0 / D)
    centre_q = jnp.sum(jnp.where(eye, centre_row, 0.0), axis=1, keepdims=True)

    gq = dot2(jnp.concatenate([dscore, weight], axis=0), right, 0, 0) * (g * SCALE)
    gp = dot2(dscore, eq, 1, 0) * (g * SCALE)
    arrived(ibuf.at[pl.ds(0, DP - 1)], INV)
    inv = ibuf[:, 0, :]
    hq = inv[:, 0:1] * (gq - nq * centre_q)
    hp = inv[:, 64:65] * (gp - np_ * centre_p)
    gh = jnp.concatenate([hq, hp], axis=0)

    @pl.when(relay != j)
    def _():
        arrived(at_buf, RELAY)

    at = at_buf[...]
    gh_hi = gh.astype(BF16)
    gh_lo = (gh - gh_hi.astype(F32)).astype(BF16)
    grad_out[...] = dot(at, gh_hi, 1, 0) + dot(at, gh_lo, 1, 0)

    sent(rcv1.at[0, pl.ds(0, FS - 1)], ATTN)
    sent(rcv1.at[1, pl.ds(0, FS - 1)], RESID)
    sent(bbuf.at[pl.ds(0, DP - 1)], BANK)
    sent(cbuf, PAIR)
    sent(ybuf.at[pl.ds(0, SIDE - 1)], YSUM)
    sent(sq, SQ)
    sent(nbuf.at[pl.ds(0, DP - 1)], NORM)
    sent(ibuf.at[pl.ds(0, DP - 1)], INV)
    sent(cb4, SPAIR)
    sent(yb4.at[pl.ds(0, SIDE - 1)], SY)
    sent(tot.at[0], SBACK)

    @pl.loop(0, 4)
    def _(t):
        @pl.when(4 * j + t != i)
        def _():
            sent(asrc, COLS)

    @pl.when(relay == j)
    def _():
        @pl.loop(0, FS - 1)
        def _(t):
            sent(at_buf, RELAY)


def on_device(attn, resid, lengths, out_proj, norm_gain, bank, hard_ids):
    any_spec = pl.BlockSpec(memory_space=pl.ANY)
    vmem = pltpu.VMEM
    loss, grad = pl.pallas_call(
        kernel,
        name="infonce",
        out_shape=(
            jax.ShapeDtypeStruct((1, 1), F32),
            jax.ShapeDtypeStruct((64, BLK), F32),
        ),
        in_specs=[any_spec] * 7,
        out_specs=(pl.BlockSpec(memory_space=vmem), pl.BlockSpec(memory_space=vmem)),
        scratch_shapes=[
            vmem((2, 64, D), BF16),
            vmem((2, 64, D), BF16),
            pltpu.SMEM((1, 2), jnp.int32),
            vmem((BLK, D), BF16),
            vmem((1, D), F32),
            vmem((2, D), BF16),
            vmem((8, 64), jnp.int32),
            vmem((2, FS, 4, 128), F32),
            vmem((2, FS, 4, 128), F32),
            vmem((16, BLK), F32),
            vmem((2, SIDE, 4, 128), F32),
            vmem((SIDE, 4, 128), F32),
            vmem((SIDE, 4, 128), F32),
            vmem((SIDE, SIDE, 4, 128), F32),
            vmem((SIDE, 4, 128), F32),
            vmem((4, 128), F32),
            vmem((4, 128), F32),
            vmem((4, 128), F32),
            vmem((DP, 4, 128), F32),
            vmem((1, 128), F32),
            vmem((DP, 1, 128), F32),
            vmem((4, 128), F32),
            vmem((DP, 4, 128), F32),
            vmem((4, 128), F32),
            vmem((DP, 4, 128), F32),
            vmem((128, 128), BF16),
            vmem((64, 128), BF16),
            vmem((2, 5, 4, 128), F32),
            vmem((5, 4, 128), F32),
            vmem((5, 4, 128), F32),
            vmem((SIDE, 5, 4, 128), F32),
            vmem((2, 5, 4, 128), F32),
            vmem((40, 128), F32),
            pltpu.SemaphoreType.DMA((7,)),
            pltpu.SemaphoreType.DMA((KINDS,)),
            pltpu.SemaphoreType.DMA((KINDS,)),
        ],
        compiler_params=pltpu.CompilerParams(
            collective_id=0, has_side_effects=True, vmem_limit_bytes=62 * 2**20
        ),
        cost_estimate=pl.CostEstimate(flops=10**8, bytes_accessed=4 * 2**20, transcendentals=10**4),
    )(attn, resid, lengths, out_proj, norm_gain.reshape(1, D), bank, hard_ids.T)
    return (loss[0, 0], grad)


def solution(mesh):
    placed = (
        P("dp", None, "fsdp", None),
        P("dp", None, "fsdp", None),
        P("dp", None),
        P("fsdp", None),
        P(),
        P("dp", None),
        P(),
    )
    return jax.shard_map(
        on_device, mesh=mesh, in_specs=placed, out_specs=(P(), P("dp", "fsdp")), check_vma=False
    )
```

time: 482 us -> 59.3 us (0.12)
  waiting for transfers between devices: 335 us -> 0 us
  blocking collectives: 103 us -> 0 us
  Pallas kernels: 0 us -> 55.2 us
  matrix products: 14.6 us -> 0 us
  between operations: 16.3 us -> 2.39 us
  local copies, waits for them, and re-layouts: 6.38 us -> 1.47 us
    reduce_scatter x1 -> x0, waiting for transfers between devices: 249 us -> none  [on_device(): lax.psum_scatter(jnp.dot(attn_float.T, grad_cols, precision=lax.Precision...]
    psum x2 -> x0, blocking collectives: 103 us -> none  [the longest x1 56.8 us: on_device(): lax.psum(own_attn, 'fsdp').astype(jnp.float32)]
    all_gather x2 -> x0, waiting for transfers between devices: 85.4 us -> none  [the longest x1 85.4 us: on_device(): lax.all_gather(embedded, 'dp', axis=0, tiled=True)]
    pallas_call x0 -> x1, Pallas kernels: none -> 55.2 us  [on_device(): pl.pallas_call(kernel, name='infonce', out_shape=(jax.ShapeDtypeStruct((1...]
    dot_general x11 -> x0, matrix products: 14.6 us -> none  [the longest x1 3.79 us: on_device(): jnp.dot(attn_float.T, grad_cols, precision=lax.Precision.HIGHEST)]
  transfers between devices with their start and end apart: 3 -> 0, of which waited for: 2 -> 0; matrix products, arithmetic and copies ran while one was open for 1% -> 0% of each run, Pallas kernels for 0% -> 0%
where the time goes in v1:
time: 59.3 us; the launch traced here: 59.1 us
  Pallas kernels  55.2 us (93%)
  between operations  2.39 us (4%)
  local copies, waits for them, and re-layouts  1.47 us (2%)
    pallas_call x1, Pallas kernels, on_device(): pl.pallas_call(kernel, name='infonce', out_shape=(jax.ShapeDtypeStruct((1...  55.2 us
    unnamed x1, local copies, waits for them, and re-layouts  1.47 us

profile of v1, /device:TPU:1, one launch (start us, length us, event | category | flops | bytes accessed | tf_op | source)
XLA Modules:
  0.0 59.1 jit_solution(17081594435552636957)
XLA Ops:
  0.6 55.2 %infonce.1 = (f32[1,1]{1,0:T(1,128)}, f32[64,256]{1,0:T(8,128)}) custom-call(bf16[1,2,64,4096]{3,2,1,0:T(8,128)(2,1)} %attn.1, bf16[1,2,64,4096]{3,2,1,0:T(8,128)(2,1)} %resid.1, s32[1,2]{1,0:T(1,128)} %lengths.1, bf16[256,4096]{1,0:T(8,128)(2,1)} %w.1, f32[1,4096]{1,0:T(1,128)} %bitcast.3, bf16[2,4096]{1,0:T(2,128)(2,1)} %bank.1, s32[8,64]{1,0:T(8,128)} %bitcast.4), custom_call_target="tpu_custom_call" | custom-call | flops 100000000 | bytes 4194304 | tf_op jit(solution)/shard_map/infonce/pallas_call | solution.py:337
  56.5 1.5 %copy.12 = f32[64,256]{1,0:T(8,128)} copy(f32[64,256]{1,0:T(8,128)} %get-tuple-element.9) | data formatting | bytes 131072

commit v2 on v1

--- a/solution.py
+++ b/solution.py
@@ -17,8 +17,11 @@
 SCALE = 4.0 / 64.0
 COUNT = 128.0
 
-ATTN, RESID, BANK, COLS, PAIR, YSUM, SQ, NORM, INV, RELAY, SPAIR, SY, SBACK = range(13)
-KINDS = 13
+ATTN, RESID, BANK, COLS, PAIR, YSUM, YOWN, SQ, NORM, REST, INV, RELAY, SPAIR, SY, SBACK = range(15)
+KINDS = 15
+
+
+FAR = (4, 5, 3, 6, 2, 7, 1, 0)
 
 
 def far(m):
@@ -38,9 +41,9 @@
 def kernel(
     attn, resid, lengths, w, gain, bank, ids, loss_out, grad_out,
     attn_v, resid_v, len_s, w_v, gain_v, bank_v, ids_v,
-    src1, rcv1, lhs, part, cbuf, half, ybuf, hid, sq, sqr,
+    src1, rcv1, lhs, part, cbuf, half, half_b, ybuf, yown, sq, sqr,
     nsrc, nbuf, isrc, ibuf, bsrc, bbuf, asrc, abuf, at_full, at_buf,
-    pay, cb4, half4, yb4, tot, flat, local_sem, ssem, rsem,
+    pay, cb4, half4, yb4, tot, flat, rsrc, rbuf, quad, wide, local_sem, ssem, rsem, plane,
 ):
     i = lax.axis_index("dp")
     j = lax.axis_index("fsdp")
@@ -48,16 +51,28 @@
     y, c = lax.div(j, 2), lax.rem(j, 2)
     partner = (i, 2 * y + 1 - c)
 
-    def dp_peer(t):
-        px = lax.rem(x + far(lax.div(t, SIDE)), SIDE)
-        pz = lax.rem(z + far(lax.rem(t, SIDE)), SIDE)
-        return (px * SIDE + pz, j)
-
-    def fs_index(t):
-        return 2 * lax.rem(y + far(lax.div(t, 2)), SIDE) + lax.rem(c + t + 1, 2)
-
-    def y_peer(t):
-        return (i, 2 * lax.rem(y + far(t), SIDE) + c)
+    pz = [lax.rem(z + m, SIDE) for m in FAR]
+    py = [2 * lax.rem(y + m, SIDE) for m in FAR]
+
+    def each_dp(act):
+        @pl.loop(0, SIDE - 1)
+        def _(t):
+            px = lax.rem(x + far(t), SIDE) * SIDE
+            for b in range(SIDE):
+                act((px + pz[b], j))
+
+        for b in range(SIDE - 1):
+            act((x * SIDE + pz[b], j))
+
+    def each_fs(act):
+        for b in range(SIDE - 1):
+            act(py[b] + 1 - c)
+            act(py[b] + c)
+        act(2 * y + 1 - c)
+
+    def each_y(act):
+        for b in range(SIDE - 1):
+            act((i, py[b] + c))
 
     def send(src, dst, kind, to):
         pltpu.make_async_remote_copy(
@@ -70,6 +85,13 @@
 
     def sent(ref, kind):
         pltpu.make_async_copy(ref, ref, ssem.at[kind]).wait()
+
+    def rows_of(buf):
+        wide[...] = buf[...].astype(F32)
+        return (
+            jnp.concatenate([wide[:, 0, :], wide[:, 1, :]], axis=1),
+            jnp.concatenate([wide[:, 2, :], wide[:, 3, :]], axis=1),
+        )
 
     loads = [
         pltpu.make_async_copy(a, b, local_sem.at[n])
@@ -83,13 +105,15 @@
 
     barrier = pltpu.get_barrier_semaphore()
 
-    @pl.loop(0, DP - 1)
-    def _(t):
-        pl.semaphore_signal(barrier, inc=1, device_id=dp_peer(t), device_id_type=MESH)
-
-    @pl.loop(0, FS - 1)
-    def _(t):
-        pl.semaphore_signal(barrier, inc=1, device_id=(i, fs_index(t)), device_id_type=MESH)
+    def greet(to):
+        pl.semaphore_signal(barrier, inc=1, device_id=to, device_id_type=MESH)
+
+    px = [lax.rem(x + m, SIDE) * SIDE for m in FAR]
+
+    each_fs(lambda to: greet((i, to)))
+    for b in range(SIDE - 1):
+        greet((x * SIDE + pz[b], j))
+        greet((px[b] + z, j))
 
     loads[0].wait()
     loads[1].wait()
@@ -110,44 +134,35 @@
         return jnp.where(even, block[:, :128], block[:, 128:])[0:4]
 
     for t in range(FS):
-        src1[0, t] = fold(dot(select, attn_v[:, :, t * BLK:(t + 1) * BLK].reshape(128, BLK), 1, 0))
+        src1[0, t] = fold(dot(select, attn_v[:, :, t * BLK:(t + 1) * BLK].reshape(128, BLK), 1, 0)).astype(BF16)
     rcv1[0, j] = src1[0, j]
-    pl.semaphore_wait(barrier, DP - 1 + FS - 1)
-
-    @pl.loop(0, FS - 1)
-    def _(t):
-        to = fs_index(t)
-        send(src1.at[0, to], rcv1.at[0, j], ATTN, (i, to))
-
+    pl.semaphore_wait(barrier, FS - 1 + 2 * (SIDE - 1))
+
+    each_fs(lambda to: send(src1.at[0, to], rcv1.at[0, j], ATTN, (i, to)))
+
+    for b in range(SIDE - 1):
+        pl.semaphore_signal(plane, inc=1, device_id=(px[b] + z, j), device_id_type=MESH)
     loads[2].wait()
     for t in range(FS):
-        src1[1, t] = fold(dot(select, resid_v[:, :, t * BLK:(t + 1) * BLK].reshape(128, BLK), 1, 0))
+        src1[1, t] = fold(dot(select, resid_v[:, :, t * BLK:(t + 1) * BLK].reshape(128, BLK), 1, 0)).astype(BF16)
     rcv1[1, j] = src1[1, j]
 
-    @pl.loop(0, FS - 1)
-    def _(t):
-        to = fs_index(t)
-        send(src1.at[1, to], rcv1.at[1, j], RESID, (i, to))
+    each_fs(lambda to: send(src1.at[1, to], rcv1.at[1, j], RESID, (i, to)))
 
     loads[3].wait()
     own = pl.ds(pl.multiple_of(j * BLK, BLK), BLK)
     bank_rows = bank_v[:, own].astype(F32)
-    bsrc[0:1] = bank_rows[0:1, :128]
-    bsrc[1:2] = bank_rows[0:1, 128:]
-    bsrc[2:3] = bank_rows[1:2, :128]
-    bsrc[3:4] = bank_rows[1:2, 128:]
+    for r in range(4):
+        quad[r:r + 1] = bank_rows[r // 2:r // 2 + 1, 128 * (r % 2):128 * (r % 2) + 128]
+    bsrc[...] = quad[...].astype(BF16)
     bbuf[i] = bsrc[...]
-
-    @pl.loop(0, DP - 1)
-    def _(t):
-        send(bsrc, bbuf.at[i], BANK, dp_peer(t))
 
     lhs[...] = jnp.zeros_like(lhs)
     loads[6].wait()
 
     arrived(rcv1.at[0, pl.ds(0, FS - 1)], ATTN)
-    block = jnp.sum(rcv1[0], axis=0)
-    asrc[...] = block
+    block = jnp.sum(rcv1[0].astype(F32), axis=0)
+    asrc[...] = block.astype(BF16)
     for r in range(4):
         lhs[r:r + 1, 0:128] = block[r - r % 2:r - r % 2 + 1]
         lhs[r:r + 1, 128:256] = block[r - r % 2 + 1:r - r % 2 + 2]
@@ -155,8 +170,19 @@
     for t in range(FS):
         part[t % 2, t // 2] = fold(dot(rows, w_v[:, t * BLK:(t + 1) * BLK], 1, 0))
     arrived(rcv1.at[1, pl.ds(0, FS - 1)], RESID)
-    part[c, y] = part[c, y] + jnp.sum(rcv1[1], axis=0)
+    part[c, y] = part[c, y] + jnp.sum(rcv1[1].astype(F32), axis=0)
     send(part.at[1 - c], cbuf, PAIR, partner)
+
+    arrived(cbuf, PAIR)
+    half[...] = part[c] + cbuf[...]
+    half_b[...] = half[...].astype(BF16)
+    ybuf[y] = half_b[...]
+    yown[y] = half[y]
+
+    each_y(lambda to: send(half_b, ybuf.at[y], YSUM, to))
+    for b in range(SIDE - 1):
+        send(half.at[lax.div(py[b], 2)], yown.at[y], YOWN, (i, py[b] + c))
+    pl.semaphore_wait(plane, SIDE - 1)
 
     @pl.loop(0, 4)
     def _(t):
@@ -172,13 +198,7 @@
     def _():
         abuf[i] = asrc[...]
 
-    arrived(cbuf, PAIR)
-    half[...] = part[c] + cbuf[...]
-    ybuf[y] = half[...]
-
-    @pl.loop(0, SIDE - 1)
-    def _(t):
-        send(half, ybuf.at[y], YSUM, y_peer(t))
+    each_dp(lambda to: send(bsrc, bbuf.at[i], BANK, to))
 
     loads[4].wait()
     loads[5].wait()
@@ -189,53 +209,55 @@
     bank_row = lax.broadcasted_iota(jnp.int32, (128, 64), 0)
 
     arrived(ybuf.at[pl.ds(0, SIDE - 1)], YSUM)
-    hid[...] = jnp.sum(ybuf[...], axis=0)
-    sq[...] = jnp.sum(hid[...] * hid[...], axis=0)
+    hid = jnp.sum(ybuf[...].astype(F32), axis=0)
+    sq[...] = jnp.sum(hid * hid, axis=0)
     send(sq, sqr, SQ, partner)
+    arrived(yown.at[pl.ds(0, SIDE - 1)], YOWN)
+    own_hid = jnp.sum(yown[...], axis=0)
     arrived(sqr, SQ)
     sums = jnp.sum(sq[...] + sqr[...], axis=1, keepdims=True)
     inv_q = lax.rsqrt((sums[0:1] + sums[1:2]) * (1.0 / D) + 1e-5)
     inv_p = lax.rsqrt((sums[2:3] + sums[3:4]) * (1.0 / D) + 1e-5)
     four = lax.broadcasted_iota(jnp.int32, (4, 128), 0)
-    nsrc[...] = hid[y] * jnp.where(four < 2, inv_q, inv_p)
+    g = gain_v[:, own]
+    scaled = (own_hid * jnp.where(four < 2, inv_q, inv_p)) * jnp.where(
+        lax.rem(four, 2) == 0, g[:, :128], g[:, 128:]
+    )
+    rounded = scaled.astype(BF16)
+    nsrc[...] = rounded
+    rsrc[...] = (scaled - rounded.astype(F32)).astype(BF16)
     lane = lax.broadcasted_iota(jnp.int32, (1, 128), 1)
     isrc[...] = jnp.where(lane < 64, inv_q, inv_p)
 
-    @pl.loop(0, DP - 1)
-    def _(t):
-        send(nsrc, nbuf.at[i], NORM, dp_peer(t))
+    each_dp(lambda to: send(nsrc, nbuf.at[i], NORM, to))
 
     nbuf[i] = nsrc[...]
+    rbuf[i] = rsrc[...]
     ibuf[i] = isrc[...]
 
-    @pl.loop(0, DP - 1)
-    def _(t):
-        send(isrc, ibuf.at[i], INV, dp_peer(t))
+    each_dp(lambda to: send(rsrc, rbuf.at[i], REST, to))
+    each_dp(lambda to: send(isrc, ibuf.at[i], INV, to))
 
     @pl.when(relay == j)
     def _():
         arrived(abuf.at[pl.ds(0, DP - 1)], COLS)
         low = lax.rem(i, 4) < 2
-        rows_q = jnp.where(low, abuf[:, 0, :], abuf[:, 1, :])
-        rows_p = jnp.where(low, abuf[:, 2, :], abuf[:, 3, :])
+        wide[...] = abuf[...].astype(F32)
+        rows_q = jnp.where(low, wide[:, 0, :], wide[:, 1, :])
+        rows_p = jnp.where(low, wide[:, 2, :], wide[:, 3, :])
         at_full[...] = jnp.concatenate([rows_q, rows_p], axis=0).T.astype(BF16)
         mine = pl.ds(pl.multiple_of(lax.rem(i, 2) * 64, 64), 64)
         at_buf[...] = at_full[mine, :]
 
-        @pl.loop(0, FS - 1)
-        def _(t):
-            send(at_full.at[mine], at_buf, RELAY, (i, fs_index(t)))
+        each_fs(lambda to: send(at_full.at[mine], at_buf, RELAY, (i, to)))
 
     arrived(bbuf.at[pl.ds(0, DP - 1)], BANK)
-    bank_e = jnp.concatenate([bbuf[:, 0, :], bbuf[:, 1, :]], axis=1).astype(BF16)
-    bank_o = jnp.concatenate([bbuf[:, 2, :], bbuf[:, 3, :]], axis=1).astype(BF16)
-    g = gain_v[:, own]
+    first_bank, second_bank = rows_of(bbuf)
+    bank_e, bank_o = first_bank.astype(BF16), second_bank.astype(BF16)
 
     arrived(nbuf.at[pl.ds(0, DP - 1)], NORM)
-    nq = jnp.concatenate([nbuf[:, 0, :], nbuf[:, 1, :]], axis=1)
-    np_ = jnp.concatenate([nbuf[:, 2, :], nbuf[:, 3, :]], axis=1)
-    eq = (nq * g).astype(BF16)
-    ep = (np_ * g).astype(BF16)
+    emb_q, emb_p = rows_of(nbuf)
+    eq, ep = emb_q.astype(BF16), emb_p.astype(BF16)
     right = jnp.concatenate([ep, bank_e, bank_o], axis=0)
     st = dot(right, eq, 1, 1)
     bank_st = st[64:192]
@@ -252,9 +274,18 @@
     half4[...] = pay[c] + cb4[...]
     yb4[y] = half4[...]
 
-    @pl.loop(0, SIDE - 1)
-    def _(t):
-        send(half4, yb4.at[y], SY, y_peer(t))
+    each_y(lambda to: send(half4, yb4.at[y], SY, to))
+
+    arrived(rbuf.at[pl.ds(0, DP - 1)], REST)
+    rest_q, rest_p = rows_of(rbuf)
+    inv_g = 1.0 / g
+    nq = (emb_q + rest_q) * inv_g
+    np_ = (emb_p + rest_p) * inv_g
+    arrived(ibuf.at[pl.ds(0, DP - 1)], INV)
+    inv = ibuf[:, 0, :]
+    @pl.when(relay != j)
+    def _():
+        arrived(at_buf, RELAY)
 
     arrived(yb4.at[pl.ds(0, SIDE - 1)], SY)
     tot[c] = jnp.sum(yb4[...], axis=0)
@@ -291,16 +322,9 @@
 
     gq = dot2(jnp.concatenate([dscore, weight], axis=0), right, 0, 0) * (g * SCALE)
     gp = dot2(dscore, eq, 1, 0) * (g * SCALE)
-    arrived(ibuf.at[pl.ds(0, DP - 1)], INV)
-    inv = ibuf[:, 0, :]
     hq = inv[:, 0:1] * (gq - nq * centre_q)
     hp = inv[:, 64:65] * (gp - np_ * centre_p)
     gh = jnp.concatenate([hq, hp], axis=0)
-
-    @pl.when(relay != j)
-    def _():
-        arrived(at_buf, RELAY)
-
     at = at_buf[...]
     gh_hi = gh.astype(BF16)
     gh_lo = (gh - gh_hi.astype(F32)).astype(BF16)
@@ -311,8 +335,10 @@
     sent(bbuf.at[pl.ds(0, DP - 1)], BANK)
     sent(cbuf, PAIR)
     sent(ybuf.at[pl.ds(0, SIDE - 1)], YSUM)
+    sent(yown.at[pl.ds(0, SIDE - 1)], YOWN)
     sent(sq, SQ)
     sent(nbuf.at[pl.ds(0, DP - 1)], NORM)
+    sent(rbuf.at[pl.ds(0, DP - 1)], REST)
     sent(ibuf.at[pl.ds(0, DP - 1)], INV)
     sent(cb4, SPAIR)
     sent(yb4.at[pl.ds(0, SIDE - 1)], SY)
@@ -351,24 +377,25 @@
             vmem((1, D), F32),
             vmem((2, D), BF16),
             vmem((8, 64), jnp.int32),
-            vmem((2, FS, 4, 128), F32),
-            vmem((2, FS, 4, 128), F32),
+            vmem((2, FS, 4, 128), BF16),
+            vmem((2, FS, 4, 128), BF16),
             vmem((16, BLK), F32),
             vmem((2, SIDE, 4, 128), F32),
             vmem((SIDE, 4, 128), F32),
             vmem((SIDE, 4, 128), F32),
-            vmem((SIDE, SIDE, 4, 128), F32),
+            vmem((SIDE, 4, 128), BF16),
+            vmem((SIDE, SIDE, 4, 128), BF16),
             vmem((SIDE, 4, 128), F32),
             vmem((4, 128), F32),
             vmem((4, 128), F32),
-            vmem((4, 128), F32),
-            vmem((DP, 4, 128), F32),
+            vmem((4, 128), BF16),
+            vmem((DP, 4, 128), BF16),
             vmem((1, 128), F32),
             vmem((DP, 1, 128), F32),
-            vmem((4, 128), F32),
-            vmem((DP, 4, 128), F32),
-            vmem((4, 128), F32),
-            vmem((DP, 4, 128), F32),
+            vmem((4, 128), BF16),
+            vmem((DP, 4, 128), BF16),
+            vmem((4, 128), BF16),
+            vmem((DP, 4, 128), BF16),
             vmem((128, 128), BF16),
             vmem((64, 128), BF16),
             vmem((2, 5, 4, 128), F32),
@@ -377,9 +404,14 @@
             vmem((SIDE, 5, 4, 128), F32),
             vmem((2, 5, 4, 128), F32),
             vmem((40, 128), F32),
+            vmem((4, 128), BF16),
+            vmem((DP, 4, 128), BF16),
+            vmem((4, 128), F32),
+            vmem((DP, 4, 128), F32),
             pltpu.SemaphoreType.DMA((7,)),
             pltpu.SemaphoreType.DMA((KINDS,)),
             pltpu.SemaphoreType.DMA((KINDS,)),
+            pltpu.SemaphoreType.REGULAR,
         ],
         compiler_params=pltpu.CompilerParams(
             collective_id=0, has_side_effects=True, vmem_limit_bytes=62 * 2**20

time: 59.3 us -> 54.2 us (0.914)
  Pallas kernels: 55.2 us -> 50.2 us
    pallas_call x1, Pallas kernels: 55.2 us -> 50.2 us  [on_device(): pl.pallas_call(kernel, name='infonce', out_shape=(jax.ShapeDtypeStruct((1...]
where the time goes in v2:
time: 54.2 us; the launch traced here: 54 us
  Pallas kernels  50.2 us (93%)
  between operations  2.39 us (4%)
  local copies, waits for them, and re-layouts  1.47 us (3%)
    pallas_call x1, Pallas kernels, on_device(): pl.pallas_call(kernel, name='infonce', out_shape=(jax.ShapeDtypeStruct((1...  50.2 us
    unnamed x1, local copies, waits for them, and re-layouts  1.47 us

profile of v2, /device:TPU:1, one launch (start us, length us, event | category | flops | bytes accessed | tf_op | source)
XLA Modules:
  0.0 54.0 jit_solution(9592323816964723166)
XLA Ops:
  0.6 50.2 %infonce.1 = (f32[1,1]{1,0:T(1,128)}, f32[64,256]{1,0:T(8,128)}) custom-call(bf16[1,2,64,4096]{3,2,1,0:T(8,128)(2,1)} %attn.1, bf16[1,2,64,4096]{3,2,1,0:T(8,128)(2,1)} %resid.1, s32[1,2]{1,0:T(1,128)} %lengths.1, bf16[256,4096]{1,0:T(8,128)(2,1)} %w.1, f32[1,4096]{1,0:T(1,128)} %bitcast.3, bf16[2,4096]{1,0:T(2,128)(2,1)} %bank.1, s32[8,64]{1,0:T(8,128)} %bitcast.4), custom_call_target="tpu_custom_call" | custom-call | flops 100000000 | bytes 4194304 | tf_op jit(solution)/shard_map/infonce/pallas_call | solution.py:363
  51.4 1.5 %copy.12 = f32[64,256]{1,0:T(8,128)} copy(f32[64,256]{1,0:T(8,128)} %get-tuple-element.9) | data formatting | bytes 131072

commit v3 on v2

--- a/solution.py
+++ b/solution.py
@@ -17,7 +17,7 @@
 SCALE = 4.0 / 64.0
 COUNT = 128.0
 
-ATTN, RESID, BANK, COLS, PAIR, YSUM, YOWN, SQ, NORM, REST, INV, RELAY, SPAIR, SY, SBACK = range(15)
+ATTN, RESID, BANK, COLS, WEIGHT, YSUM, YOWN, SQ, NORM, REST, INV, RELAY, SPAIR, SY, SBACK = range(15)
 KINDS = 15
 
 
@@ -41,9 +41,9 @@
 def kernel(
     attn, resid, lengths, w, gain, bank, ids, loss_out, grad_out,
     attn_v, resid_v, len_s, w_v, gain_v, bank_v, ids_v,
-    src1, rcv1, lhs, part, cbuf, half, half_b, ybuf, yown, sq, sqr,
+    src_a, rcv_a, src_r, rcv_r, pooled, lhs, half, half_b, ybuf, yown, sq, sqr,
     nsrc, nbuf, isrc, ibuf, bsrc, bbuf, asrc, abuf, at_full, at_buf,
-    pay, cb4, half4, yb4, tot, flat, rsrc, rbuf, quad, wide, local_sem, ssem, rsem, plane,
+    pay, cb4, half4, yb4, tot, flat, rsrc, rbuf, quad, wide, local_sem, w_sem, ssem, rsem, plane,
 ):
     i = lax.axis_index("dp")
     j = lax.axis_index("fsdp")
@@ -97,12 +97,16 @@
         pltpu.make_async_copy(a, b, local_sem.at[n])
         for n, (a, b) in enumerate([
             (lengths, len_s), (attn.at[0], attn_v), (resid.at[0], resid_v), (bank, bank_v),
-            (ids, ids_v), (gain, gain_v), (w, w_v),
+            (ids, ids_v), (gain, gain_v),
         ])
     ]
-    for load in loads:
-        load.start()
-
+
+    def w_block(k, parity):
+        return w.at[:, pl.ds(pl.multiple_of((2 * k + parity) * BLK, BLK), BLK)]
+
+    own_w = [
+        pltpu.make_async_copy(w_block(k, c), w_v.at[c, k], w_sem.at[k]) for k in range(SIDE)
+    ]
     barrier = pltpu.get_barrier_semaphore()
 
     def greet(to):
@@ -111,9 +115,13 @@
     px = [lax.rem(x + m, SIDE) * SIDE for m in FAR]
 
     each_fs(lambda to: greet((i, to)))
+    for load in loads[:2]:
+        load.start()
     for b in range(SIDE - 1):
         greet((x * SIDE + pz[b], j))
         greet((px[b] + z, j))
+    for load in loads[2:] + own_w:
+        load.start()
 
     loads[0].wait()
     loads[1].wait()
@@ -134,20 +142,26 @@
         return jnp.where(even, block[:, :128], block[:, 128:])[0:4]
 
     for t in range(FS):
-        src1[0, t] = fold(dot(select, attn_v[:, :, t * BLK:(t + 1) * BLK].reshape(128, BLK), 1, 0)).astype(BF16)
-    rcv1[0, j] = src1[0, j]
+        src_a[t // 2, t % 2] = fold(
+            dot(select, attn_v[:, :, t * BLK:(t + 1) * BLK].reshape(128, BLK), 1, 0)
+        ).astype(BF16)
+    rcv_a[j] = src_a[y]
     pl.semaphore_wait(barrier, FS - 1 + 2 * (SIDE - 1))
 
-    each_fs(lambda to: send(src1.at[0, to], rcv1.at[0, j], ATTN, (i, to)))
+    each_fs(lambda to: send(src_a.at[lax.div(to, 2)], rcv_a.at[j], ATTN, (i, to)))
+    for k in range(SIDE):
+        send(w_block(k, 1 - c), w_v.at[c, k], WEIGHT, partner)
 
     for b in range(SIDE - 1):
         pl.semaphore_signal(plane, inc=1, device_id=(px[b] + z, j), device_id_type=MESH)
     loads[2].wait()
     for t in range(FS):
-        src1[1, t] = fold(dot(select, resid_v[:, :, t * BLK:(t + 1) * BLK].reshape(128, BLK), 1, 0)).astype(BF16)
-    rcv1[1, j] = src1[1, j]
-
-    each_fs(lambda to: send(src1.at[1, to], rcv1.at[1, j], RESID, (i, to)))
+        src_r[t] = fold(
+            dot(select, resid_v[:, :, t * BLK:(t + 1) * BLK].reshape(128, BLK), 1, 0)
+        ).astype(BF16)
+    rcv_r[j] = src_r[j]
+
+    each_fs(lambda to: send(src_r.at[to], rcv_r.at[j], RESID, (i, to)))
 
     loads[3].wait()
     own = pl.ds(pl.multiple_of(j * BLK, BLK), BLK)
@@ -158,23 +172,22 @@
     bbuf[i] = bsrc[...]
 
     lhs[...] = jnp.zeros_like(lhs)
-    loads[6].wait()
-
-    arrived(rcv1.at[0, pl.ds(0, FS - 1)], ATTN)
-    block = jnp.sum(rcv1[0].astype(F32), axis=0)
-    asrc[...] = block.astype(BF16)
-    for r in range(4):
-        lhs[r:r + 1, 0:128] = block[r - r % 2:r - r % 2 + 1]
-        lhs[r:r + 1, 128:256] = block[r - r % 2 + 1:r - r % 2 + 2]
+    for load in own_w:
+        load.wait()
+
+    arrived(rcv_a.at[pl.ds(0, FS - 1)], ATTN)
+    pooled[...] = jnp.sum(rcv_a[...].astype(F32), axis=0)
+    for b in range(2):
+        for r in range(4):
+            pick_r = r - r % 2
+            lhs[r:r + 1, BLK * b:BLK * b + 128] = pooled[b, pick_r:pick_r + 1]
+            lhs[r:r + 1, BLK * b + 128:BLK * (b + 1)] = pooled[b, pick_r + 1:pick_r + 2]
     rows = lhs[...].astype(BF16)
-    for t in range(FS):
-        part[t % 2, t // 2] = fold(dot(rows, w_v[:, t * BLK:(t + 1) * BLK], 1, 0))
-    arrived(rcv1.at[1, pl.ds(0, FS - 1)], RESID)
-    part[c, y] = part[c, y] + jnp.sum(rcv1[1].astype(F32), axis=0)
-    send(part.at[1 - c], cbuf, PAIR, partner)
-
-    arrived(cbuf, PAIR)
-    half[...] = part[c] + cbuf[...]
+    arrived(w_v.at[0], WEIGHT)
+    for k in range(SIDE):
+        half[k] = fold(dot(rows[:, :BLK], w_v[0, k], 1, 0) + dot(rows[:, BLK:], w_v[1, k], 1, 0))
+    arrived(rcv_r.at[pl.ds(0, FS - 1)], RESID)
+    half[y] = half[y] + jnp.sum(rcv_r[...].astype(F32), axis=0)
     half_b[...] = half[...].astype(BF16)
     ybuf[y] = half_b[...]
     yown[y] = half[y]
@@ -182,6 +195,7 @@
     each_y(lambda to: send(half_b, ybuf.at[y], YSUM, to))
     for b in range(SIDE - 1):
         send(half.at[lax.div(py[b], 2)], yown.at[y], YOWN, (i, py[b] + c))
+    asrc[...] = pooled[c].astype(BF16)
     pl.semaphore_wait(plane, SIDE - 1)
 
     @pl.loop(0, 4)
@@ -330,10 +344,10 @@
     gh_lo = (gh - gh_hi.astype(F32)).astype(BF16)
     grad_out[...] = dot(at, gh_hi, 1, 0) + dot(at, gh_lo, 1, 0)
 
-    sent(rcv1.at[0, pl.ds(0, FS - 1)], ATTN)
-    sent(rcv1.at[1, pl.ds(0, FS - 1)], RESID)
+    sent(rcv_a.at[pl.ds(0, FS - 1)], ATTN)
+    sent(w_v.at[0], WEIGHT)
+    sent(rcv_r.at[pl.ds(0, FS - 1)], RESID)
     sent(bbuf.at[pl.ds(0, DP - 1)], BANK)
-    sent(cbuf, PAIR)
     sent(ybuf.at[pl.ds(0, SIDE - 1)], YSUM)
     sent(yown.at[pl.ds(0, SIDE - 1)], YOWN)
     sent(sq, SQ)
@@ -373,15 +387,16 @@
             vmem((2, 64, D), BF16),
             vmem((2, 64, D), BF16),
             pltpu.SMEM((1, 2), jnp.int32),
-            vmem((BLK, D), BF16),
+            vmem((2, SIDE, BLK, BLK), BF16),
             vmem((1, D), F32),
             vmem((2, D), BF16),
             vmem((8, 64), jnp.int32),
-            vmem((2, FS, 4, 128), BF16),
-            vmem((2, FS, 4, 128), BF16),
-            vmem((16, BLK), F32),
-            vmem((2, SIDE, 4, 128), F32),
-            vmem((SIDE, 4, 128), F32),
+            vmem((SIDE, 2, 4, 128), BF16),
+            vmem((FS, 2, 4, 128), BF16),
+            vmem((FS, 4, 128), BF16),
+            vmem((FS, 4, 128), BF16),
+            vmem((2, 4, 128), F32),
+            vmem((16, 2 * BLK), F32),
             vmem((SIDE, 4, 128), F32),
             vmem((SIDE, 4, 128), BF16),
             vmem((SIDE, SIDE, 4, 128), BF16),
@@ -408,7 +423,8 @@
             vmem((DP, 4, 128), BF16),
             vmem((4, 128), F32),
             vmem((DP, 4, 128), F32),
-            pltpu.SemaphoreType.DMA((7,)),
+            pltpu.SemaphoreType.DMA((6,)),
+            pltpu.SemaphoreType.DMA((SIDE,)),
             pltpu.SemaphoreType.DMA((KINDS,)),
             pltpu.SemaphoreType.DMA((KINDS,)),
             pltpu.SemaphoreType.REGULAR,

time: 54.2 us -> 53.6 us (0.989)
  Pallas kernels: 50.2 us -> 49.5 us
    pallas_call x1, Pallas kernels: 50.2 us -> 49.5 us  [on_device(): pl.pallas_call(kernel, name='infonce', out_shape=(jax.ShapeDtypeStruct((1...]
where the time goes in v3:
time: 53.6 us; the launch traced here: 53.4 us
  Pallas kernels  49.5 us (92%)
  between operations  2.39 us (4%)
  local copies, waits for them, and re-layouts  1.47 us (3%)
    pallas_call x1, Pallas kernels, on_device(): pl.pallas_call(kernel, name='infonce', out_shape=(jax.ShapeDtypeStruct((1...  49.5 us
    unnamed x1, local copies, waits for them, and re-layouts  1.47 us

profile of v3, /device:TPU:1, one launch (start us, length us, event | category | flops | bytes accessed | tf_op | source)
XLA Modules:
  0.0 53.4 jit_solution(18068234121953171309)
XLA Ops:
  0.6 49.5 %infonce.1 = (f32[1,1]{1,0:T(1,128)}, f32[64,256]{1,0:T(8,128)}) custom-call(bf16[1,2,64,4096]{3,2,1,0:T(8,128)(2,1)} %attn.1, bf16[1,2,64,4096]{3,2,1,0:T(8,128)(2,1)} %resid.1, s32[1,2]{1,0:T(1,128)} %lengths.1, bf16[256,4096]{1,0:T(8,128)(2,1)} %w.1, f32[1,4096]{1,0:T(1,128)} %bitcast.3, bf16[2,4096]{1,0:T(2,128)(2,1)} %bank.1, s32[8,64]{1,0:T(8,128)} %bitcast.4), custom_call_target="tpu_custom_call" | custom-call | flops 100000000 | bytes 4194304 | tf_op jit(solution)/shard_map/infonce/pallas_call | solution.py:377
  50.8 1.5 %copy.12 = f32[64,256]{1,0:T(8,128)} copy(f32[64,256]{1,0:T(8,128)} %get-tuple-element.9) | data formatting | bytes 131072
